TPU v7x, 512 devices: a whole 4x4x16 slice. The times are simulated.
512 devices in a mesh: var: 32 (over x, z_lo), smp: 16 (over z_hi, y, core).
Axes of the slice: x: 4, y: 4, z: 16 (z_hi: 2, z_lo: 8; z = z_hi * 8 + z_lo), core: 2. Of those that a mesh axis runs over, the one named last changes fastest.
Arguments:
- dosages: bfloat16 [8192, 16384], P('var', 'smp'), may hold values from 0 to 2
- band_counts: int32 [64], P('var'), may hold values from 512 to 2048, as said below
Outputs:
- upper: float32 [8192, 2048], P('var', 'smp')
- lower: float32 [8192, 2048], P('var', 'smp')
Inputs may be any that keep to these rules, and one draw needn't show every extreme that they name: `band_counts`: every value lies in 512 to 2048; both ends are taken by some block.
All inputs are finite; a program needn't handle non-finite values.
Results may differ from a plain program's by a relative error of at most 0.0005.
The roundings to bfloat16 on the way count: a program that leaves them out, or rounds other values in their place, can miss the bound.
Values may be sent and summed in bfloat16 or wider, within the bound.
A program may use at most 64 MiB of HBM per device.

v0:
```python
import jax
import jax.numpy as jnp
from jax import lax
from jax.sharding import PartitionSpec as P

W = 2048
BLK = 128


def passed_along(block, axis, distance):
    devices = range(lax.axis_size(axis))
    route = [(i - distance, i) for i in devices if i - distance in devices]
    return lax.ppermute(block, axis, route)


def skew_forward(products, span):
    count, width = products.shape
    flat = jnp.concatenate([products.reshape(-1), jnp.zeros((count + 1,), jnp.float32)])
    return flat[1 : 1 + count * (width + 1)].reshape(count, width + 1)[:, :span]


def skew_backward(products, span):
    count, width = products.shape
    flat = products[:, ::-1].reshape(-1)
    return flat[count : count + count * (width - 1)].reshape(count, width - 1)[:, :span]


def contract(left, right):
    return lax.dot_general(
        left, right, (((1,), (1,)), ((), ())), preferred_element_type=jnp.float32
    )


def per_device(dosages, band_counts):
    rows, cols = dosages.shape
    depth = -(-W // rows)
    total_samples = cols * lax.axis_size("smp")
    total_rows = rows * lax.axis_size("var")
    first = lax.axis_index("var") * rows
    values = dosages.astype(jnp.float32)
    means = lax.psum(jnp.sum(values, axis=1, keepdims=True), "smp") / total_samples
    centred = values - means
    spread = lax.psum(jnp.sum(centred * centred, axis=1, keepdims=True), "smp") / total_samples
    scaled = (centred * lax.rsqrt(spread + 1e-05)).astype(jnp.bfloat16)
    later = [passed_along(scaled, "var", -step) for step in range(1, depth + 1)]
    partners = jnp.concatenate([scaled] + later, 0)
    products = contract(scaled, partners) / total_samples
    width = partners.shape[0]
    row_ids = lax.broadcasted_iota(jnp.int32, (rows, width), 0)
    col_ids = lax.broadcasted_iota(jnp.int32, (rows, width), 1)
    row_counts = jnp.repeat(band_counts, BLK)[:, None]
    offset = col_ids - row_ids - 1
    keep = (offset >= 0) & (offset < row_counts) & (first + col_ids < total_rows)
    upper_terms = skew_forward(jnp.where(keep, products, jnp.float32(0.0)), W)
    upper = lax.psum_scatter(upper_terms, "smp", scatter_dimension=1, tiled=True)
    earlier = [passed_along((scaled, band_counts), "var", step) for step in range(depth, 0, -1)]
    behind = jnp.concatenate([pair[0] for pair in earlier] + [scaled], 0)
    behind_counts = jnp.concatenate([pair[1] for pair in earlier] + [band_counts], 0)
    column_counts = jnp.repeat(behind_counts, BLK)[None, :]
    backward = contract(scaled, behind) / total_samples
    back_offset = depth * rows + row_ids - 1 - col_ids
    back_keep = (back_offset >= 0) & (back_offset < column_counts)
    lower_terms = skew_backward(jnp.where(back_keep, backward, jnp.float32(0.0)), W)
    lower = lax.psum_scatter(lower_terms, "smp", scatter_dimension=1, tiled=True)
    return (upper, lower)


def solution(mesh):
    return jax.shard_map(
        per_device,
        mesh=mesh,
        in_specs=(P("var", "smp"), P("var")),
        out_specs=(P("var", "smp"), P("var", "smp")),
        check_vma=False,
    )
```

profile of v0, /device:TPU:6, one launch (start us, length us, event | category | flops | bytes accessed | tf_op | source)
XLA Modules:
  0.0 845.7 jit_solution(17809763496074444488)
XLA Ops:
  8.4 77.8 %psum.14 = f32[256,1]{0,1:T(1,128)S(1)} all-reduce(f32[256,1]{0,1:T(1,128)S(1)} %bitcast.15), channel_id=1, replica_groups=mesh['var'=32,'smp'=16] {'smp'}, use_global_device_ids=true, to_apply=%region_1.0 | all-reduce | flops 256 | bytes 2048 | tf_op jit(solution)/shard_map/psum | solution.py:41
  87.5 62.0 %psum.15 = f32[256,1]{0,1:T(1,128)S(1)} all-reduce(f32[256,1]{0,1:T(1,128)S(1)} %bitcast.16), channel_id=1, replica_groups=mesh['var'=32,'smp'=16] {'smp'}, use_global_device_ids=true, to_apply=%region_3.0 | all-reduce | flops 256 | bytes 2048 | tf_op jit(solution)/shard_map/psum | solution.py:43
  149.5 2.0 constant_dynamic-update-slice_fusion.8
  151.5 5.8 collective-permute-start
  157.4 2.6 collective-permute-start.1
  160.0 4.0 collective-permute-start.2
  164.0 5.1 collective-permute-start.3
  169.1 2.1 collective-permute-start.4
  172.0 5.5 collective-permute-start.5
  178.3 13.2 %collective-permute-done.1 = bf16[256,1024]{1,0:T(8,128)(2,1)S(1)} collective-permute-done((bf16[256,1024]{1,0:T(8,128)(2,1)S(1)}, bf16[256,1024]{1,0:T(8,128)(2,1)S(1)}, u32[]{:S(2)}, u32[]{:S(2)}) %collective-permute-start.1) | collective-permute-done | bytes 524320 | tf_op jit(solution)/shard_map/ppermute | solution.py:13
  191.5 48.2 %collective-permute-start.6 = (bf16[256,1024]{1,0:T(8,128)(2,1)S(1)}, bf16[256,1024]{1,0:T(8,128)(2,1)S(1)}, u32[]{:S(2)}, u32[]{:S(2)}) collective-permute-start(bf16[256,1024]{1,0:T(8,128)(2,1)S(1)} %get-tuple-element.3), channel_id=1, source_target_pairs={{112,0},{128,16},{144,32},{160,48},{176,64},{192,80},{208,96},{224... | collective-permute-start | bytes 1572872 | tf_op jit(solution)/shard_map/ppermute | solution.py:13
  240.5 2.5 collective-permute-start.7
  243.8 94.4 %collective-permute-done.3 = bf16[256,1024]{1,0:T(8,128)(2,1)S(1)} collective-permute-done((bf16[256,1024]{1,0:T(8,128)(2,1)S(1)}, bf16[256,1024]{1,0:T(8,128)(2,1)S(1)}, u32[]{:S(2)}, u32[]{:S(2)}) %collective-permute-start.3) | collective-permute-done | bytes 524320 | tf_op jit(solution)/shard_map/ppermute | solution.py:13
  342.4 4.2 fusion
  346.6 1.6 reshape.18
  348.2 2.3 pad_slice_fusion
  350.5 3.3 reshape.19
  353.8 3.2 slice.16
  358.4 1.9 collective-permute-start.17
  360.3 1.9 collective-permute-start.18
  362.2 2.5 collective-permute-start.19
  366.1 28.2 %collective-permute-done.8 = s32[2]{0:T(128)S(1)} collective-permute-done((s32[2]{0:T(128)S(1)}, s32[2]{0:T(128)S(1)}, u32[]{:S(2)}, u32[]{:S(2)}) %collective-permute-start.8) | collective-permute-done | bytes 40 | tf_op jit(solution)/shard_map/ppermute | solution.py:13
  394.3 1.9 collective-permute-start.9
  396.2 4.4 collective-permute-done.9
  400.6 1.9 collective-permute-start.10
  402.6 20.5 %collective-permute-done.10 = s32[2]{0:T(128)S(1)} collective-permute-done((s32[2]{0:T(128)S(1)}, s32[2]{0:T(128)S(1)}, u32[]{:S(2)}, u32[]{:S(2)}) %collective-permute-start.10) | collective-permute-done | bytes 40 | tf_op jit(solution)/shard_map/ppermute | solution.py:13
  423.0 8.1 collective-permute-start.11
  431.1 22.4 %collective-permute-done.11 = s32[2]{0:T(128)S(1)} collective-permute-done((s32[2]{0:T(128)S(1)}, s32[2]{0:T(128)S(1)}, u32[]{:S(2)}, u32[]{:S(2)}) %collective-permute-start.11) | collective-permute-done | bytes 40 | tf_op jit(solution)/shard_map/ppermute | solution.py:13
  453.5 1.9 collective-permute-start.12
  455.4 10.4 %collective-permute-done.12 = s32[2]{0:T(128)S(1)} collective-permute-done((s32[2]{0:T(128)S(1)}, s32[2]{0:T(128)S(1)}, u32[]{:S(2)}, u32[]{:S(2)}) %collective-permute-start.12) | collective-permute-done | bytes 40 | tf_op jit(solution)/shard_map/ppermute | solution.py:13
  465.8 9.1 %collective-permute-start.13 = (s32[2]{0:T(128)S(1)}, s32[2]{0:T(128)S(1)}, u32[]{:S(2)}, u32[]{:S(2)}) collective-permute-start(s32[2]{0:T(128)S(1)} %copy-done), channel_id=1, source_target_pairs={{0,48},{16,64},{32,80},{48,96},{64,112},{80,128},{96,144},{112,160... | collective-permute-start | bytes 32 | tf_op jit(solution)/shard_map/ppermute | solution.py:13
  474.9 6.3 collective-permute-done.13
  481.2 4.5 collective-permute-start.14
  485.7 7.5 collective-permute-done.14
  493.2 1.9 collective-permute-start.15
  495.1 11.2 %collective-permute-done.15 = s32[2]{0:T(128)S(1)} collective-permute-done((s32[2]{0:T(128)S(1)}, s32[2]{0:T(128)S(1)}, u32[]{:S(2)}, u32[]{:S(2)}) %collective-permute-start.15) | collective-permute-done | bytes 40 | tf_op jit(solution)/shard_map/ppermute | solution.py:13
  506.3 1.9 collective-permute-start.20
  508.4 1.9 collective-permute-start.21
  510.4 1.9 collective-permute-start.22
  512.4 2.1 collective-permute-start.23
  514.6 103.2 %collective-permute-done.20 = bf16[256,1024]{1,0:T(8,128)(2,1)S(1)} collective-permute-done((bf16[256,1024]{1,0:T(8,128)(2,1)S(1)}, bf16[256,1024]{1,0:T(8,128)(2,1)S(1)}, u32[]{:S(2)}, u32[]{:S(2)}) %collective-permute-start.20) | collective-permute-done | bytes 524320 | tf_op jit(solution)/shard_map/ppermute | solution.py:13
  618.0 3.0 fusion.1
  621.1 16.8 %rev.3 = f32[256,2304]{1,0:T(8,128)S(1)} reverse(f32[256,2304]{1,0:T(8,128)} %fusion.1), dimensions={1} | reverse | bytes 4718592 | tf_op jit(solution)/shard_map/rev | solution.py:24
  637.9 1.5 reshape.20
  639.4 1.8 slice.17
  641.2 3.3 reshape.21
  644.5 3.1 slice.18
  647.7 191.2 %reduce-scatter.5.cloned.1.call-done = f32[256,128]{1,0:T(8,128)} async-done(((f32[256,2048]{1,0:T(8,128)}), f32[256,128]{1,0:T(8,128)}) %reduce-scatter.5.cloned.1.call-update) | async-done | bytes 131088 | tf_op jit(solution)/shard_map/reduce_scatter | solution.py:64
  (48 shorter events, 13.2 us)
Async XLA Ops:
  7.2 640.5 %reduce-scatter.3.cloned.1.call-start = ((), (), s32[]{:S(2)}) async-start(), calls=%async_computation.2 | async-start | bytes 2228224 | tf_op jit(solution)/shard_map/reduce_scatter | solution.py:55
  151.5 20.5 %collective-permute-start = (bf16[256,1024]{1,0:T(8,128)(2,1)S(1)}, bf16[256,1024]{1,0:T(8,128)(2,1)S(1)}, u32[]{:S(2)}, u32[]{:S(2)}) collective-permute-start(bf16[256,1024]{1,0:T(8,128)(2,1)S(1)} %get-tuple-element.3), channel_id=1, source_target_pairs={{16,0},{32,16},{48,32},{64,48},{80,64},{96,80},{112,96},{128,112},... | collective-permute-start | bytes 1572872 | tf_op jit(solution)/shard_map/ppermute | solution.py:13
  157.4 34.1 %collective-permute-start.1 = (bf16[256,1024]{1,0:T(8,128)(2,1)S(1)}, bf16[256,1024]{1,0:T(8,128)(2,1)S(1)}, u32[]{:S(2)}, u32[]{:S(2)}) collective-permute-start(bf16[256,1024]{1,0:T(8,128)(2,1)S(1)} %get-tuple-element.3), channel_id=1, source_target_pairs={{32,0},{48,16},{64,32},{80,48},{96,64},{112,80},{128,96},{144,112}... | collective-permute-start | bytes 1572872 | tf_op jit(solution)/shard_map/ppermute | solution.py:13
  160.0 80.6 %collective-permute-start.2 = (bf16[256,1024]{1,0:T(8,128)(2,1)S(1)}, bf16[256,1024]{1,0:T(8,128)(2,1)S(1)}, u32[]{:S(2)}, u32[]{:S(2)}) collective-permute-start(bf16[256,1024]{1,0:T(8,128)(2,1)S(1)} %get-tuple-element.3), channel_id=1, source_target_pairs={{48,0},{64,16},{80,32},{96,48},{112,64},{128,80},{144,96},{160,112... | collective-permute-start | bytes 1572872 | tf_op jit(solution)/shard_map/ppermute | solution.py:13
  164.0 174.2 %collective-permute-start.3 = (bf16[256,1024]{1,0:T(8,128)(2,1)S(1)}, bf16[256,1024]{1,0:T(8,128)(2,1)S(1)}, u32[]{:S(2)}, u32[]{:S(2)}) collective-permute-start(bf16[256,1024]{1,0:T(8,128)(2,1)S(1)} %get-tuple-element.3), channel_id=1, source_target_pairs={{64,0},{80,16},{96,32},{112,48},{128,64},{144,80},{160,96},{176,11... | collective-permute-start | bytes 1572872 | tf_op jit(solution)/shard_map/ppermute | solution.py:13
  169.1 169.9 %collective-permute-start.4 = (bf16[256,1024]{1,0:T(8,128)(2,1)S(1)}, bf16[256,1024]{1,0:T(8,128)(2,1)S(1)}, u32[]{:S(2)}, u32[]{:S(2)}) collective-permute-start(bf16[256,1024]{1,0:T(8,128)(2,1)S(1)} %get-tuple-element.3), channel_id=1, source_target_pairs={{80,0},{96,16},{112,32},{128,48},{144,64},{160,80},{176,96},{192,1... | collective-permute-start | bytes 1572872 | tf_op jit(solution)/shard_map/ppermute | solution.py:13
  172.0 167.9 %collective-permute-start.5 = (bf16[256,1024]{1,0:T(8,128)(2,1)S(1)}, bf16[256,1024]{1,0:T(8,128)(2,1)S(1)}, u32[]{:S(2)}, u32[]{:S(2)}) collective-permute-start(bf16[256,1024]{1,0:T(8,128)(2,1)S(1)} %get-tuple-element.3), channel_id=1, source_target_pairs={{96,0},{112,16},{128,32},{144,48},{160,64},{176,80},{192,96},{208,... | collective-permute-start | bytes 1572872 | tf_op jit(solution)/shard_map/ppermute | solution.py:13
  191.5 149.3 %collective-permute-start.6 = (bf16[256,1024]{1,0:T(8,128)(2,1)S(1)}, bf16[256,1024]{1,0:T(8,128)(2,1)S(1)}, u32[]{:S(2)}, u32[]{:S(2)}) collective-permute-start(bf16[256,1024]{1,0:T(8,128)(2,1)S(1)} %get-tuple-element.3), channel_id=1, source_target_pairs={{112,0},{128,16},{144,32},{160,48},{176,64},{192,80},{208,96},{224... | collective-permute-start | bytes 1572872 | tf_op jit(solution)/shard_map/ppermute | solution.py:13
  240.5 101.0 %collective-permute-start.7 = (bf16[256,1024]{1,0:T(8,128)(2,1)S(1)}, bf16[256,1024]{1,0:T(8,128)(2,1)S(1)}, u32[]{:S(2)}, u32[]{:S(2)}) collective-permute-start(bf16[256,1024]{1,0:T(8,128)(2,1)S(1)} %get-tuple-element.3), channel_id=1, source_target_pairs={{128,0},{144,16},{160,32},{176,48},{192,64},{208,80},{224,96},{240... | collective-permute-start | bytes 1572872 | tf_op jit(solution)/shard_map/ppermute | solution.py:13
  350.5 14.2 %copy-start = (s32[2]{0:T(128)S(1)}, s32[2]{0:T(128)}, u32[]{:S(2)}) copy-start(s32[2]{0:T(128)} %param.3) | copy-start | bytes 28
  357.0 481.8 %reduce-scatter.5.cloned.1.call-start = ((), (), s32[]{:S(2)}) async-start(), calls=%async_computation.3 | async-start | bytes 2228224 | tf_op jit(solution)/shard_map/reduce_scatter | solution.py:64
  357.1 151.4 %collective-permute-start.16 = (bf16[256,1024]{1,0:T(8,128)(2,1)S(1)}, bf16[256,1024]{1,0:T(8,128)(2,1)S(1)}, u32[]{:S(2)}, u32[]{:S(2)}) collective-permute-start(bf16[256,1024]{1,0:T(8,128)(2,1)S(1)} %get-tuple-element.3), channel_id=1, source_target_pairs={{0,128},{16,144},{32,160},{48,176},{64,192},{80,208},{96,224},{112... | collective-permute-start | bytes 1572872 | tf_op jit(solution)/shard_map/ppermute | solution.py:13
  358.4 152.0 %collective-permute-start.17 = (bf16[256,1024]{1,0:T(8,128)(2,1)S(1)}, bf16[256,1024]{1,0:T(8,128)(2,1)S(1)}, u32[]{:S(2)}, u32[]{:S(2)}) collective-permute-start(bf16[256,1024]{1,0:T(8,128)(2,1)S(1)} %get-tuple-element.3), channel_id=1, source_target_pairs={{0,112},{16,128},{32,144},{48,160},{64,176},{80,192},{96,208},{112... | collective-permute-start | bytes 1572872 | tf_op jit(solution)/shard_map/ppermute | solution.py:13
  360.3 152.1 %collective-permute-start.18 = (bf16[256,1024]{1,0:T(8,128)(2,1)S(1)}, bf16[256,1024]{1,0:T(8,128)(2,1)S(1)}, u32[]{:S(2)}, u32[]{:S(2)}) collective-permute-start(bf16[256,1024]{1,0:T(8,128)(2,1)S(1)} %get-tuple-element.3), channel_id=1, source_target_pairs={{0,96},{16,112},{32,128},{48,144},{64,160},{80,176},{96,192},{112,... | collective-permute-start | bytes 1572872 | tf_op jit(solution)/shard_map/ppermute | solution.py:13
  362.2 152.3 %collective-permute-start.19 = (bf16[256,1024]{1,0:T(8,128)(2,1)S(1)}, bf16[256,1024]{1,0:T(8,128)(2,1)S(1)}, u32[]{:S(2)}, u32[]{:S(2)}) collective-permute-start(bf16[256,1024]{1,0:T(8,128)(2,1)S(1)} %get-tuple-element.3), channel_id=1, source_target_pairs={{0,80},{16,96},{32,112},{48,128},{64,144},{80,160},{96,176},{112,1... | collective-permute-start | bytes 1572872 | tf_op jit(solution)/shard_map/ppermute | solution.py:13
  364.8 29.5 %collective-permute-start.8 = (s32[2]{0:T(128)S(1)}, s32[2]{0:T(128)S(1)}, u32[]{:S(2)}, u32[]{:S(2)}) collective-permute-start(s32[2]{0:T(128)S(1)} %copy-done), channel_id=1, source_target_pairs={{0,128},{16,144},{32,160},{48,176},{64,192},{80,208},{96,224},{112... | collective-permute-start | bytes 32 | tf_op jit(solution)/shard_map/ppermute | solution.py:13
  394.3 6.3 collective-permute-start.9
  400.6 22.4 %collective-permute-start.10 = (s32[2]{0:T(128)S(1)}, s32[2]{0:T(128)S(1)}, u32[]{:S(2)}, u32[]{:S(2)}) collective-permute-start(s32[2]{0:T(128)S(1)} %copy-done), channel_id=1, source_target_pairs={{0,96},{16,112},{32,128},{48,144},{64,160},{80,176},{96,192},{112,... | collective-permute-start | bytes 32 | tf_op jit(solution)/shard_map/ppermute | solution.py:13
  423.0 30.4 %collective-permute-start.11 = (s32[2]{0:T(128)S(1)}, s32[2]{0:T(128)S(1)}, u32[]{:S(2)}, u32[]{:S(2)}) collective-permute-start(s32[2]{0:T(128)S(1)} %copy-done), channel_id=1, source_target_pairs={{0,80},{16,96},{32,112},{48,128},{64,144},{80,160},{96,176},{112,1... | collective-permute-start | bytes 32 | tf_op jit(solution)/shard_map/ppermute | solution.py:13
  453.5 12.3 %collective-permute-start.12 = (s32[2]{0:T(128)S(1)}, s32[2]{0:T(128)S(1)}, u32[]{:S(2)}, u32[]{:S(2)}) collective-permute-start(s32[2]{0:T(128)S(1)} %copy-done), channel_id=1, source_target_pairs={{0,64},{16,80},{32,96},{48,112},{64,128},{80,144},{96,160},{112,17... | collective-permute-start | bytes 32 | tf_op jit(solution)/shard_map/ppermute | solution.py:13
  465.8 15.4 %collective-permute-start.13 = (s32[2]{0:T(128)S(1)}, s32[2]{0:T(128)S(1)}, u32[]{:S(2)}, u32[]{:S(2)}) collective-permute-start(s32[2]{0:T(128)S(1)} %copy-done), channel_id=1, source_target_pairs={{0,48},{16,64},{32,80},{48,96},{64,112},{80,128},{96,144},{112,160... | collective-permute-start | bytes 32 | tf_op jit(solution)/shard_map/ppermute | solution.py:13
  481.2 12.1 %collective-permute-start.14 = (s32[2]{0:T(128)S(1)}, s32[2]{0:T(128)S(1)}, u32[]{:S(2)}, u32[]{:S(2)}) collective-permute-start(s32[2]{0:T(128)S(1)} %copy-done), channel_id=1, source_target_pairs={{0,32},{16,48},{32,64},{48,80},{64,96},{80,112},{96,128},{112,144}... | collective-permute-start | bytes 32 | tf_op jit(solution)/shard_map/ppermute | solution.py:13
  493.2 13.1 %collective-permute-start.15 = (s32[2]{0:T(128)S(1)}, s32[2]{0:T(128)S(1)}, u32[]{:S(2)}, u32[]{:S(2)}) collective-permute-start(s32[2]{0:T(128)S(1)} %copy-done), channel_id=1, source_target_pairs={{0,16},{16,32},{32,48},{48,64},{64,80},{80,96},{96,112},{112,128},... | collective-permute-start | bytes 32 | tf_op jit(solution)/shard_map/ppermute | solution.py:13
  506.3 111.5 %collective-permute-start.20 = (bf16[256,1024]{1,0:T(8,128)(2,1)S(1)}, bf16[256,1024]{1,0:T(8,128)(2,1)S(1)}, u32[]{:S(2)}, u32[]{:S(2)}) collective-permute-start(bf16[256,1024]{1,0:T(8,128)(2,1)S(1)} %get-tuple-element.3), channel_id=1, source_target_pairs={{0,64},{16,80},{32,96},{48,112},{64,128},{80,144},{96,160},{112,17... | collective-permute-start | bytes 1572872 | tf_op jit(solution)/shard_map/ppermute | solution.py:13
  508.4 109.4 %collective-permute-start.21 = (bf16[256,1024]{1,0:T(8,128)(2,1)S(1)}, bf16[256,1024]{1,0:T(8,128)(2,1)S(1)}, u32[]{:S(2)}, u32[]{:S(2)}) collective-permute-start(bf16[256,1024]{1,0:T(8,128)(2,1)S(1)} %get-tuple-element.3), channel_id=1, source_target_pairs={{0,48},{16,64},{32,80},{48,96},{64,112},{80,128},{96,144},{112,160... | collective-permute-start | bytes 1572872 | tf_op jit(solution)/shard_map/ppermute | solution.py:13
  510.4 107.5 %collective-permute-start.22 = (bf16[256,1024]{1,0:T(8,128)(2,1)S(1)}, bf16[256,1024]{1,0:T(8,128)(2,1)S(1)}, u32[]{:S(2)}, u32[]{:S(2)}) collective-permute-start(bf16[256,1024]{1,0:T(8,128)(2,1)S(1)} %get-tuple-element.3), channel_id=1, source_target_pairs={{0,32},{16,48},{32,64},{48,80},{64,96},{80,112},{96,128},{112,144}... | collective-permute-start | bytes 1572872 | tf_op jit(solution)/shard_map/ppermute | solution.py:13
  512.4 105.6 %collective-permute-start.23 = (bf16[256,1024]{1,0:T(8,128)(2,1)S(1)}, bf16[256,1024]{1,0:T(8,128)(2,1)S(1)}, u32[]{:S(2)}, u32[]{:S(2)}) collective-permute-start(bf16[256,1024]{1,0:T(8,128)(2,1)S(1)} %get-tuple-element.3), channel_id=1, source_target_pairs={{0,16},{16,32},{32,48},{48,64},{64,80},{80,96},{96,112},{112,128},... | collective-permute-start | bytes 1572872 | tf_op jit(solution)/shard_map/ppermute | solution.py:13
Sparse Core Ops, SparseCore 0:
  357.1 264.7 reduce-scatter.2
  647.8 191.0 reduce-scatter.4
where the time goes:
time: 848 us; the launch traced here: 846 us
  waiting for transfers between devices  513 us (60%)
  blocking collectives  140 us (17%)
  starting transfers between devices  122 us (14%)
  local copies, waits for them, and re-layouts  44.8 us (5%)
  between operations  14.4 us (2%)
    ppermute x24, waiting for transfers between devices, passed_along(): return lax.ppermute(block, axis, route)  322 us
    reduce_scatter x1, waiting for transfers between devices, per_device(): lax.psum_scatter(lower_terms, 'smp', scatter_dimension=1, tiled=True)  191 us
    ppermute x24, starting transfers between devices, passed_along(): return lax.ppermute(block, axis, route)  122 us
    psum x1, blocking collectives, per_device(): lax.psum(jnp.sum(values, axis=1, keepdims=True), 'smp') / total_samples  77.8 us
    psum x1, blocking collectives, per_device(): lax.psum(jnp.sum(centred * centred, axis=1, keepdims=True), 'smp')  62 us
  transfers between devices with their start and end apart: 26, of which 12 were waited for; matrix products, arithmetic and copies ran while one was open for 4% of the time, Pallas kernels for 0%

commit v1 on v0

v1 whole, which is shorter than its diff:
```python
import functools

import jax
import jax.numpy as jnp
from jax import lax
from jax.experimental import pallas as pl
from jax.experimental.pallas import tpu as pltpu
from jax.sharding import PartitionSpec as P

W = 2048
BLK = 128
LINE = 8
YS = 4
CHUNKS = 4
FOLD, GIVE, TAKE = 1, 3, 6
MESH = pl.DeviceIdType.MESH


def skew(tile):
    n = tile.shape[1]
    sub = lax.broadcasted_iota(jnp.int32, (8, n), 0)
    parts = []
    for at in range(0, tile.shape[0], 8):
        part = pltpu.roll(tile[at : at + 8], (2 * n - at - 1) % n, 1)
        for step in (1, 2, 4):
            part = jnp.where((sub & step) != 0, pltpu.roll(part, n - step, 1), part)
        parts.append(part)
    return jnp.concatenate(parts, 0)


def unshear(window, rows):
    height, n = window.shape
    lag = n - 1 - lax.broadcasted_iota(jnp.int32, (height, n), 1)
    step = 1
    while step < n:
        moved = pltpu.roll(window, height - step, 0)
        window = jnp.where((lag & step) != 0, moved, window)
        step *= 2
    return window[:rows]


DOWN, UP, BACK, FORE = range(4)
ONE_ON, TWO_ON, HIGH_ON, BEHIND = 8, 9, 10, 11
SLOTS = 12
REACH = 9
PHASES = 4
TASKS = 16


def kernel(
    total_samples, total_rows,
    dosages, counts, upper, lower,
    raw, ready, mine, twin, shares, part, other, across, arrived, window, stat_out, stat_in, facts,
    stat_ss, stat_rs, raw_ss, raw_rs, fact_ss, fact_rs,
    twin_ss, twin_rs, share_ss, share_rs, give_ss, give_rs, end_ss, end_rs,
):
    rows, cols = dosages.shape
    v = lax.axis_index("var")
    s = lax.axis_index("smp")
    x, z = v // LINE, v % LINE
    hi, y, core = s // (2 * YS), (s // 2) % YS, s % 2
    lines = total_rows // rows // LINE
    blocks = lines * LINE
    mid = LINE // 2
    smps = 4 * YS
    group = hi * YS + y
    chunk = rows // CHUNKS
    width = upper.shape[1]
    f32 = jnp.float32
    low = z < mid
    first_line, last_line = x == 0, x == lines - 1
    pick = jnp.where

    def there(d):
        return (d != 0) & (v + d >= 0) & (v + d < blocks)

    barrier = pltpu.get_barrier_semaphore()
    for step in range(smps // 2, smps + smps // 2):
        if step != smps:
            peer = lax.rem(s + step, smps)
            pl.semaphore_signal(barrier, inc=1, device_id=(v, peer), device_id_type=MESH)

    def greet(n, carry):
        d = n - REACH

        @pl.when(there(d))
        def _():
            pl.semaphore_signal(barrier, inc=1, device_id=(v + d, s), device_id_type=MESH)

        return carry

    lax.fori_loop(0, 2 * REACH + 1, greet, 0)
    neighbours = jnp.minimum(v, REACH) + jnp.minimum(blocks - 1 - v, REACH)

    def send(way, slot, to_slot, k, src=None):
        at = pl.ds(k * chunk, chunk)
        to = (v - 1, v + 1, v - LINE, v + LINE)[way]
        return pltpu.make_async_remote_copy(
            src_ref=raw.at[slot, at] if src is None else src.at[at], dst_ref=raw.at[to_slot, at],
            send_sem=raw_ss.at[way, slot, k], recv_sem=raw_rs.at[to_slot, k],
            device_id=(to, s), device_id_type=MESH)

    def receive(slot, k):
        send(DOWN, slot, slot, k).wait_recv()

    def own_sends(k, act):
        @pl.when(low)
        def _():
            act(send(UP, z, z, k, dosages))

        @pl.when(~low)
        def _():
            act(send(DOWN, z, z, k, dosages))

        @pl.when(~first_line & ((z == 0) | ((z >= mid) & (z < LINE - 1))))
        def _():
            act(send(BACK, z, ONE_ON, k, dosages))

        @pl.when(~last_line & (z > 0))
        def _():
            act(send(FORE, z, BEHIND, k, dosages))

    def from_above(i):
        return jnp.maximum(z + 1, mid) + i

    def from_below(i):
        return jnp.minimum(z, mid) - 1 - i

    def relay(i, k, act, wait):
        above, below = from_above(i), from_below(i)

        @pl.when((i < mid) & (above < LINE))
        def _():
            if wait:
                receive(above, k)

            @pl.when(z > 0)
            def _():
                act(send(DOWN, above, above, k))

            @pl.when(~first_line & (z >= mid) & (i == 0))
            def _():
                act(send(BACK, above, TWO_ON, k))

        @pl.when((i < mid) & (below >= 0))
        def _():
            if wait:
                receive(below, k)

            @pl.when(z < LINE - 1)
            def _():
                act(send(UP, below, below, k))

            @pl.when(~first_line & low & (below == 0))
            def _():
                act(send(BACK, below, ONE_ON, k))

            @pl.when(~first_line & (z == mid) & (i == 0))
            def _():
                act(send(BACK, below, HIGH_ON, k))

    def start(copy):
        copy.start()

    def sent(copy):
        copy.wait_send()

    def local_statistics():
        values = dosages[...].astype(f32)
        local_mean = jnp.sum(values, axis=1, keepdims=True) / cols
        centred = values - local_mean
        local_m2 = jnp.sum(centred * centred, axis=1, keepdims=True)
        lane = lax.broadcasted_iota(jnp.int32, (rows, 128), 1)
        both = jnp.where(lane == 0, local_mean, jnp.where(lane == 1, local_m2, f32(0.0)))
        stat_out[...] = both.T[0:2, :]

    local_statistics()
    pl.semaphore_wait(barrier, neighbours + smps - 1)

    for k in range(CHUNKS):
        own_sends(k, start)

    def stat_copy(step):
        peer = lax.rem(s + step, smps)
        return pltpu.make_async_remote_copy(
            src_ref=stat_out, dst_ref=stat_in.at[step], send_sem=stat_ss.at[step],
            recv_sem=stat_rs.at[step], device_id=(v, peer), device_id_type=MESH)

    for step in range(1, smps):
        stat_copy(step).start()
    stat_in[0] = stat_out[...]

    def needed(at, d):
        spot = at + d
        inside = pick(at < mid, (d < 0) | (spot >= mid), (d > 0) | (spot < mid))
        after = pick(
            at < mid,
            spot == LINE,
            (at < LINE - 1) & ((d == LINE) | (d == LINE + 1) | ((d == LINE - 1) & (at == mid))),
        )
        return pick(spot < 0, (d == -LINE) & (at > 0), pick(spot >= LINE, after, inside))

    def fact_copy(d):
        return pltpu.make_async_remote_copy(
            src_ref=facts.at[REACH], dst_ref=facts.at[REACH - d], send_sem=fact_ss.at[REACH + d],
            recv_sem=fact_rs.at[REACH - d], device_id=(v + d, s), device_id_type=MESH)

    def each_fact(act):
        def one(n, carry):
            d = n - REACH

            @pl.when(there(d) & needed((v + d + LINE) % LINE, -d))
            def _():
                act(fact_copy(d))

            return carry

        lax.fori_loop(0, 2 * REACH + 1, one, 0)

    def column(at, k):
        line_id = lax.broadcasted_iota(jnp.int32, (128, rows), 0)
        table = facts[at]
        flat = jnp.where(line_id == 0, table[k[0] : k[0] + 1], f32(0.0))
        for j in range(1, len(k)):
            flat = jnp.where(line_id == j, table[k[j] : k[j] + 1], flat)
        return flat.T

    def standardize(block, slot, d):
        flat = column(REACH + d, (0, 1))
        scaled = (block[...].astype(f32) - flat[:, 0:1]) * flat[:, 1:2]
        ready[slot] = scaled.astype(jnp.bfloat16)

    def settle():
        for step in range(1, smps):
            stat_copy(step).wait()
        gathered = stat_in[...]
        local_means = gathered[:, 0, :]
        mean = jnp.sum(local_means, axis=0, keepdims=True) / smps
        off = local_means - mean
        m2 = jnp.sum(gathered[:, 1, :] + cols * (off * off), axis=0, keepdims=True)
        place = lax.broadcasted_iota(jnp.int32, (3, rows), 0)
        scale = lax.rsqrt(m2 / total_samples + 1e-05)
        facts[REACH] = jnp.where(place == 0, mean, jnp.where(place == 1, scale, counts[...]))
        each_fact(start)
        standardize(dosages, z, 0)

        @pl.when(last_line)
        def _():
            ready[ONE_ON] = jnp.zeros((rows, cols), jnp.bfloat16)

    def take_in(slot, d, whole):
        if whole:
            for k in range(CHUNKS):
                receive(slot, k)
        fact_copy(-d).wait_recv()
        standardize(raw.at[slot], slot, d)

    def prepare(step):
        @pl.when((step < mid) & (from_above(step) < LINE))
        def _():
            take_in(from_above(step), from_above(step) - z, False)

        @pl.when((step < mid) & (from_below(step) >= 0))
        def _():
            take_in(from_below(step), from_below(step) - z, False)

        @pl.when((step == 1) & ~first_line & (z > 0))
        def _():
            take_in(BEHIND, -LINE, True)

        @pl.when((step == 2) & ~last_line & (z >= mid) & (z < LINE - 1))
        def _():
            take_in(ONE_ON, LINE, True)
            take_in(TWO_ON, LINE + 1, True)

        @pl.when((step == 2) & ~last_line & (z == mid))
        def _():
            take_in(HIGH_ON, LINE - 1, True)

        @pl.when((step == 3) & ~last_line & low)
        def _():
            take_in(ONE_ON, LINE - z, True)

    def task(family, i):
        if family == 0:
            left = jnp.maximum(z, mid) + i
            at = pick(low, jnp.minimum(i + 1, 3), i)
            return low | (i <= LINE - 2 - z), at, z, left, left + 1, left - z, i * 0
        if family == 1:
            left = jnp.minimum(z, mid - 1) - 1 - i
            return (left >= 0) & ~first_line, i + 1, BEHIND, left, left + 1, LINE + left - z, i * 0 - LINE
        if family == 2:
            holds = pick(low, i <= z - 1, (i <= LINE - 2 - z) & ~last_line)
            return (
                holds, pick(low, i, 2 + i // 2), pick(low, z - 1 - i, z + 1 + i), pick(low, z - 1, ONE_ON),
                pick(low, z, TWO_ON), pick(low, i, LINE - 1 - i), pick(low, -1 - i, 1 + i))
        below, at = z == mid - 1, z == mid
        end = ((z == 1) & (i < 2)) | ((z == 2) & (i >= 2))
        return (
            below | (at & ~last_line) | end, pick(below, i, pick(at, 2 + i // 2, 3)),
            pick(below, mid - 1 - i, mid + i), pick(below, mid - 1, pick(at, HIGH_ON, LINE - 1)),
            pick(below, mid, ONE_ON), pick(below, i, pick(at, LINE - 1 - i, mid - 1 - i)),
            pick(below, -i, pick(at, i, mid + i - z)))

    row_ids = lax.broadcasted_iota(jnp.int32, (rows, rows), 0)
    col_ids = lax.broadcasted_iota(jnp.int32, (rows, rows), 1)

    def multiply(left, right):
        return lax.dot_general(
            ready[left], ready[right], (((1,), (1,)), ((), ())), preferred_element_type=f32
        )

    def twin_copy(n):
        return pltpu.make_async_remote_copy(
            src_ref=other.at[n], dst_ref=twin.at[n], send_sem=twin_ss.at[n], recv_sem=twin_rs.at[n],
            device_id=(v, s + 1 - 2 * core), device_id_type=MESH)

    def run(n, row, left, right):
        merged = jnp.where(col_ids > row_ids, multiply(row, left), multiply(row, right))
        turned = skew(merged)
        first, second = turned[:, :width], turned[:, width:]

        @pl.when(core == 0)
        def _():
            mine[n] = first
            other[n] = second

        @pl.when(core != 0)
        def _():
            mine[n] = second
            other[n] = first

        twin_copy(n).start()

    def share_copy(n, g):
        peer = hi * (2 * YS) + lax.rem(g, YS) * 2 + core
        return pltpu.make_async_remote_copy(
            src_ref=mine.at[n], dst_ref=shares.at[n, y], send_sem=share_ss.at[n],
            recv_sem=share_rs.at[n, y], device_id=(v, peer), device_id_type=MESH)

    def fold(n, g):
        twin_copy(n).wait_recv()
        both = mine[n] + twin[n]

        @pl.when(lax.rem(g, YS) == y)
        def _():
            shares[n, y] = both

        @pl.when(lax.rem(g, YS) != y)
        def _():
            mine[n] = both
            share_copy(n, g).start()

    def gather(n):
        for step in range(1, YS):
            source = lax.rem(y + step, YS)
            pltpu.make_async_remote_copy(
                src_ref=shares.at[n, source], dst_ref=shares.at[n, source], send_sem=share_ss.at[n],
                recv_sem=share_rs.at[n, source], device_id=(v, s), device_id_type=MESH).wait_recv()
        return jnp.sum(shares[n], axis=0)

    def give_copy(n):
        return pltpu.make_async_remote_copy(
            src_ref=part.at[n], dst_ref=across.at[n], send_sem=give_ss.at[n], recv_sem=give_rs.at[n],
            device_id=(v, (1 - hi) * (2 * YS) + y * 2 + core), device_id_type=MESH)

    def give(n):
        part[n] = gather(n)
        give_copy(n).start()

    step_rows = rows // 2
    full_at = pl.ds(pl.multiple_of((1 - core) * step_rows, step_rows), rows)
    half_at = pl.ds(pl.multiple_of(core * rows, step_rows), step_rows)
    half_rows = pl.ds(pl.multiple_of((1 - core) * step_rows, step_rows), step_rows)

    def ends(n, far):
        places = []
        for j, (d, src, dst) in enumerate(
            (
                (far, part.at[n], arrived),
                (far + group + core, part.at[n], window.at[full_at]),
                (far + group + 1 - core, part.at[n, half_rows], window.at[half_at]),
            )
        ):
            copy = pltpu.make_async_remote_copy(
                src_ref=src, dst_ref=dst, send_sem=end_ss.at[n, j], recv_sem=end_rs.at[j],
                device_id=(v + d, s), device_id_type=MESH)
            places.append((d, copy))
        return places

    def take(n, far):
        total = gather(n)
        give_copy(n).wait_recv()
        total = (total + across[n]) / total_samples
        offset = lax.broadcasted_iota(jnp.int32, (rows, width), 1) + s * width
        later = lax.broadcasted_iota(jnp.int32, (rows, width), 0) + (v + far) * rows + 1 + offset
        count = column(REACH + far, (2,))[:, 0:1]
        keep = (offset.astype(f32) < count) & (later < total_rows)
        part[n] = jnp.where(keep, total, f32(0.0))
        up_to, full_to, half_to = ends(n, far)

        @pl.when(up_to[0] == 0)
        def _():
            arrived[...] = part[n]

        @pl.when(full_to[0] == 0)
        def _():
            window[full_at, :] = part[n]

        @pl.when(half_to[0] == 0)
        def _():
            window[half_at, :] = part[n, half_rows, :]

        for d, copy in (up_to, full_to, half_to):

            @pl.when(there(d))
            def _(copy=copy):
                copy.start()

    def work(phase, step):
        def each(stage, family, when):
            def one(i, carry):
                holds, at, row, left, right, g, far = task(family, i)
                n = family * mid + i
                due = holds & (at == when)
                if stage == 0:

                    @pl.when(due)
                    def _():
                        run(n, row, left, right)

                if stage == 1:

                    @pl.when(due)
                    def _():
                        fold(n, g)

                if stage == 2:

                    @pl.when(due & (lax.rem(g, YS) == y) & (g // YS != hi))
                    def _():
                        give(n)

                if stage == 3:

                    @pl.when(due & (g == group))
                    def _():
                        take(n, far)

                return carry

            lax.fori_loop(0, mid, one, 0)

        for stage, lag in enumerate((0, FOLD, GIVE, TAKE)):
            slot = phase - lag
            each(stage, slot % PHASES, step + slot // PHASES)

    early = (z < 2) | (z >= LINE - 2)

    @pl.when(early)
    def _():
        settle()

    for k in range(CHUNKS):
        relay(0, k, start, True)

    @pl.when(~early)
    def _():
        settle()

    def stream(t, carry):
        for phase in range(PHASES):
            for k in range(phase * CHUNKS // PHASES, (phase + 1) * CHUNKS // PHASES):
                relay(t, k, start, True)
            if phase == 0:
                prepare(t - 1)
            work(phase, t - 1)
        return carry

    lax.fori_loop(1, 1 + (4 * PHASES + TAKE + PHASES - 1) // PHASES, stream, 0)

    local = [False, False, False]
    for family in range(4):
        for i in range(mid):
            holds, _, _, _, _, g, far = task(family, jnp.int32(i))
            for j, d in enumerate((far, far + group + core, far + group + 1 - core)):
                local[j] = local[j] | (holds & (g == group) & (d == 0))
    exists = ~last_line | (group <= LINE - 1 - z)
    full_from, half_from = v - group - core, v - group - 1 + core
    incoming = ends(0, 0)

    @pl.when(~local[0] & exists)
    def _():
        incoming[0][1].wait_recv()

    @pl.when(~exists)
    def _():
        arrived[...] = jnp.zeros((rows, width), f32)

    upper[...] = arrived[...]

    @pl.when(full_from < 0)
    def _():
        window[full_at, :] = jnp.zeros((rows, width), f32)

    @pl.when(half_from < 0)
    def _():
        window[half_at, :] = jnp.zeros((step_rows, width), f32)

    @pl.when((full_from >= 0) & ~local[1])
    def _():
        incoming[1][1].wait_recv()

    @pl.when((half_from >= 0) & ~local[2])
    def _():
        incoming[2][1].wait_recv()

    lower[...] = unshear(window[...], rows)

    for k in range(CHUNKS):
        own_sends(k, sent)

    def relayed(m, carry):
        relay(m // CHUNKS, m % CHUNKS, sent, False)
        return carry

    lax.fori_loop(0, mid * CHUNKS, relayed, 0)
    each_fact(sent)

    for family in range(4):

        def moved(i, carry, family=family):
            holds, _, _, _, _, g, far = task(family, i)
            n = family * mid + i
            in_plane = lax.rem(g, YS) == y

            @pl.when(holds)
            def _():
                twin_copy(n).wait_send()

            @pl.when(holds & ~in_plane)
            def _():
                share_copy(n, g).wait_send()

            @pl.when(holds & in_plane & (g // YS != hi))
            def _():
                give_copy(n).wait_send()

            for d, copy in ends(n, far):

                @pl.when(holds & (g == group) & there(d))
                def _(copy=copy):
                    copy.wait_send()

            return carry

        lax.fori_loop(0, mid, moved, 0)


def per_device(dosages, band_counts):
    rows, cols = dosages.shape
    smps, blocks = lax.axis_size("smp"), lax.axis_size("var")
    width = W // smps
    f32 = jnp.float32
    counts = jnp.repeat(band_counts.astype(f32), BLK)[None, :]
    vmem = pl.BlockSpec(memory_space=pltpu.VMEM)
    dma = pltpu.SemaphoreType.DMA
    out = jax.ShapeDtypeStruct((rows, width), f32)
    tile = pltpu.VMEM((TASKS, rows, width), f32)
    return pl.pallas_call(
        functools.partial(kernel, cols * smps, rows * blocks),
        out_shape=(out, out),
        in_specs=[vmem, vmem],
        out_specs=(vmem, vmem),
        scratch_shapes=[
            pltpu.VMEM((SLOTS, rows, cols), jnp.bfloat16),
            pltpu.VMEM((SLOTS, rows, cols), jnp.bfloat16),
            tile,
            tile,
            pltpu.VMEM((TASKS, YS, rows, width), f32),
            tile,
            tile,
            tile,
            pltpu.VMEM((rows, width), f32),
            pltpu.VMEM((rows + rows // 2, width), f32),
            pltpu.VMEM((2, rows), f32),
            pltpu.VMEM((smps, 2, rows), f32),
            pltpu.VMEM((2 * REACH + 1, 3, rows), f32),
            dma((smps,)),
            dma((smps,)),
            dma((4, SLOTS, CHUNKS)),
            dma((SLOTS, CHUNKS)),
            dma((2 * REACH + 1,)),
            dma((2 * REACH + 1,)),
            dma((TASKS,)),
            dma((TASKS,)),
            dma((TASKS,)),
            dma((TASKS, YS)),
            dma((TASKS,)),
            dma((TASKS,)),
            dma((TASKS, 3)),
            dma((3,)),
        ],
        compiler_params=pltpu.CompilerParams(
            collective_id=0, has_side_effects=True, vmem_limit_bytes=56 * 2**20
        ),
        cost_estimate=pl.CostEstimate(
            flops=2 * rows * (W + rows) * cols, bytes_accessed=rows * cols * 2, transcendentals=0
        ),
    )(dosages, counts)


def solution(mesh):
    return jax.shard_map(
        per_device,
        mesh=mesh,
        in_specs=(P("var", "smp"), P("var")),
        out_specs=(P("var", "smp"), P("var", "smp")),
        check_vma=False,
    )
```

time: 848 us -> 143 us (0.17)
  the two profiles are of different devices: /device:TPU:6 before, /device:TPU:20 now
where the time goes in v1:
time: 143 us
  Pallas kernels  139 us (97%)
  local copies, waits for them, and re-layouts  2.9 us (2%)
    pallas_call x1, Pallas kernels, per_device(): pl.pallas_call(functools.partial(kernel, cols * smps, rows * blocks), out...  139 us

profile of v1, /device:TPU:20, one launch (start us, length us, event | category | flops | bytes accessed | tf_op | source)
XLA Modules:
  0.0 142.7 jit_solution(7024876255928694170)
XLA Ops:
  0.6 0.7 convert_element_type.3
  1.3 0.6 broadcast_in_dim.3
  1.9 138.5 %shard_map.41 = (f32[256,128]{1,0:T(8,128)}, f32[256,128]{1,0:T(8,128)}) custom-call(bf16[256,1024]{1,0:T(8,128)(2,1)} %dosages.1, f32[1,256]{1,0:T(1,128)} %bitcast.1), custom_call_target="tpu_custom_call" | custom-call | flops 1207959552 | bytes 524288 | tf_op jit(solution)/shard_map/pallas_call | solution.py:570
  140.4 0.0 copy-start
  140.4 1.6 %copy.6 = f32[256,128]{1,0:T(8,128)} copy(f32[256,128]{1,0:T(8,128)} %get-tuple-element.4) | data formatting | bytes 262144
  142.0 0.0 copy-done
  142.1 0.7 copy.7
Async XLA Ops:
  140.4 1.6 %copy-start = (f32[256,128]{1,0:T(8,128)S(1)}, f32[256,128]{1,0:T(8,128)}, u32[]{:S(2)}) copy-start(f32[256,128]{1,0:T(8,128)} %get-tuple-element.5) | copy-start | bytes 393220

commit v2 on v1

--- a/solution.py
+++ b/solution.py
@@ -11,8 +11,9 @@
 BLK = 128
 LINE = 8
 YS = 4
-CHUNKS = 4
+CHUNKS = 8
 FOLD, GIVE, TAKE = 1, 3, 6
+BEHIND_BY = 2
 MESH = pl.DeviceIdType.MESH
 
 
@@ -50,7 +51,7 @@
 def kernel(
     total_samples, total_rows,
     dosages, counts, upper, lower,
-    raw, ready, mine, twin, shares, part, other, across, arrived, window, stat_out, stat_in, facts,
+    raw, ready, mine, twin, shares, part, other, across, arrived, window, stat_out, stat_in, stat_sum, facts,
     stat_ss, stat_rs, raw_ss, raw_rs, fact_ss, fact_rs,
     twin_ss, twin_rs, share_ss, share_rs, give_ss, give_rs, end_ss, end_rs,
 ):
@@ -62,8 +63,8 @@
     lines = total_rows // rows // LINE
     blocks = lines * LINE
     mid = LINE // 2
-    smps = 4 * YS
     group = hi * YS + y
+    plane = y * 2 + core
     chunk = rows // CHUNKS
     width = upper.shape[1]
     f32 = jnp.float32
@@ -74,11 +75,14 @@
     def there(d):
         return (d != 0) & (v + d >= 0) & (v + d < blocks)
 
+    def plane_peer(step):
+        return (v, hi * (2 * YS) + lax.rem(plane + step, 2 * YS))
+
     barrier = pltpu.get_barrier_semaphore()
-    for step in range(smps // 2, smps + smps // 2):
-        if step != smps:
-            peer = lax.rem(s + step, smps)
-            pl.semaphore_signal(barrier, inc=1, device_id=(v, peer), device_id_type=MESH)
+    across_peer = (v, (1 - hi) * (2 * YS) + plane)
+    pl.semaphore_signal(barrier, inc=1, device_id=across_peer, device_id_type=MESH)
+    for step in range(1, 2 * YS):
+        pl.semaphore_signal(barrier, inc=1, device_id=plane_peer(step), device_id_type=MESH)
 
     def greet(n, carry):
         d = n - REACH
@@ -174,21 +178,38 @@
         both = jnp.where(lane == 0, local_mean, jnp.where(lane == 1, local_m2, f32(0.0)))
         stat_out[...] = both.T[0:2, :]
 
-    local_statistics()
-    pl.semaphore_wait(barrier, neighbours + smps - 1)
+    pl.semaphore_wait(barrier, neighbours + 2 * YS)
 
     for k in range(CHUNKS):
         own_sends(k, start)
 
+    local_statistics()
+
     def stat_copy(step):
-        peer = lax.rem(s + step, smps)
         return pltpu.make_async_remote_copy(
             src_ref=stat_out, dst_ref=stat_in.at[step], send_sem=stat_ss.at[step],
-            recv_sem=stat_rs.at[step], device_id=(v, peer), device_id_type=MESH)
-
-    for step in range(1, smps):
+            recv_sem=stat_rs.at[step], device_id=plane_peer(step), device_id_type=MESH)
+
+    def far_stat():
+        return pltpu.make_async_remote_copy(
+            src_ref=stat_sum.at[0], dst_ref=stat_sum.at[1], send_sem=stat_ss.at[0],
+            recv_sem=stat_rs.at[0], device_id=across_peer, device_id_type=MESH)
+
+    def pooled(table, samples):
+        means = table[:, 0, :]
+        mean = jnp.sum(means, axis=0, keepdims=True) / table.shape[0]
+        off = means - mean
+        return mean, jnp.sum(table[:, 1, :] + samples * (off * off), axis=0, keepdims=True)
+
+    place = lax.broadcasted_iota(jnp.int32, (3, rows), 0)
+    for step in range(1, 2 * YS):
         stat_copy(step).start()
     stat_in[0] = stat_out[...]
+    for step in range(1, 2 * YS):
+        stat_copy(step).wait()
+    plane_mean, plane_m2 = pooled(stat_in[...], cols)
+    stat_sum[0] = jnp.where(place[:2] == 0, plane_mean, plane_m2)
+    far_stat().start()
 
     def needed(at, d):
         spot = at + d
@@ -231,14 +252,8 @@
         ready[slot] = scaled.astype(jnp.bfloat16)
 
     def settle():
-        for step in range(1, smps):
-            stat_copy(step).wait()
-        gathered = stat_in[...]
-        local_means = gathered[:, 0, :]
-        mean = jnp.sum(local_means, axis=0, keepdims=True) / smps
-        off = local_means - mean
-        m2 = jnp.sum(gathered[:, 1, :] + cols * (off * off), axis=0, keepdims=True)
-        place = lax.broadcasted_iota(jnp.int32, (3, rows), 0)
+        far_stat().wait()
+        mean, m2 = pooled(stat_sum[...], cols * 2 * YS)
         scale = lax.rsqrt(m2 / total_samples + 1e-05)
         facts[REACH] = jnp.where(place == 0, mean, jnp.where(place == 1, scale, counts[...]))
         each_fact(start)
@@ -362,7 +377,7 @@
     def give_copy(n):
         return pltpu.make_async_remote_copy(
             src_ref=part.at[n], dst_ref=across.at[n], send_sem=give_ss.at[n], recv_sem=give_rs.at[n],
-            device_id=(v, (1 - hi) * (2 * YS) + y * 2 + core), device_id_type=MESH)
+            device_id=across_peer, device_id_type=MESH)
 
     def give(n):
         part[n] = gather(n)
@@ -417,67 +432,36 @@
             def _(copy=copy):
                 copy.start()
 
+    def sweep(stage, family, due):
+        def one(i, carry):
+            holds, at, row, left, right, g, far = task(family, i)
+            n = family * mid + i
+            now = holds & due(at * PHASES + family)
+            if stage == 1:
+                now = now & (lax.rem(g, YS) == y) & (g // YS != hi)
+            if stage == 2:
+                now = now & (g == group)
+
+            @pl.when(now)
+            def _():
+                if stage == -1:
+                    run(n, row, left, right)
+                if stage == 0:
+                    fold(n, g)
+                if stage == 1:
+                    give(n)
+                if stage == 2:
+                    take(n, far)
+
+            return carry
+
+        lax.fori_loop(0, mid, one, 0)
+
     def work(phase, step):
-        def each(stage, family, when):
-            def one(i, carry):
-                holds, at, row, left, right, g, far = task(family, i)
-                n = family * mid + i
-                due = holds & (at == when)
-                if stage == 0:
-
-                    @pl.when(due)
-                    def _():
-                        run(n, row, left, right)
-
-                if stage == 1:
-
-                    @pl.when(due)
-                    def _():
-                        fold(n, g)
-
-                if stage == 2:
-
-                    @pl.when(due & (lax.rem(g, YS) == y) & (g // YS != hi))
-                    def _():
-                        give(n)
-
-                if stage == 3:
-
-                    @pl.when(due & (g == group))
-                    def _():
-                        take(n, far)
-
-                return carry
-
-            lax.fori_loop(0, mid, one, 0)
-
         for stage, lag in enumerate((0, FOLD, GIVE, TAKE)):
-            slot = phase - lag
-            each(stage, slot % PHASES, step + slot // PHASES)
-
-    early = (z < 2) | (z >= LINE - 2)
-
-    @pl.when(early)
-    def _():
-        settle()
-
-    for k in range(CHUNKS):
-        relay(0, k, start, True)
-
-    @pl.when(~early)
-    def _():
-        settle()
-
-    def stream(t, carry):
-        for phase in range(PHASES):
-            for k in range(phase * CHUNKS // PHASES, (phase + 1) * CHUNKS // PHASES):
-                relay(t, k, start, True)
-            if phase == 0:
-                prepare(t - 1)
-            work(phase, t - 1)
-        return carry
-
-    lax.fori_loop(1, 1 + (4 * PHASES + TAKE + PHASES - 1) // PHASES, stream, 0)
+            family = (phase - lag) % PHASES
+            when = step * PHASES + phase - lag
+            sweep(stage - 1, family, lambda slot, when=when: slot == when)
 
     local = [False, False, False]
     for family in range(4):
@@ -485,6 +469,41 @@
             holds, _, _, _, _, g, far = task(family, jnp.int32(i))
             for j, d in enumerate((far, far + group + core, far + group + 1 - core)):
                 local[j] = local[j] | (holds & (g == group) & (d == 0))
+
+    early = (z < 2) | (z >= LINE - 2)
+
+    @pl.when(early)
+    def _():
+        settle()
+
+    for k in range(CHUNKS):
+        relay(0, k, start, True)
+
+    @pl.when(~early)
+    def _():
+        settle()
+
+    def stream(t, carry):
+        for phase in range(PHASES):
+            for k in range(phase * CHUNKS // PHASES, (phase + 1) * CHUNKS // PHASES):
+                relay(t, k, start, True)
+            step = t - 1 + (phase - BEHIND_BY) // PHASES
+            if phase == BEHIND_BY:
+                prepare(step)
+            work((phase - BEHIND_BY) % PHASES, step)
+        return carry
+
+    lax.fori_loop(1, mid, stream, 0)
+    done = (mid - 1) * PHASES - BEHIND_BY - 1
+    prepare(mid - 1)
+    for family in range(4):
+        sweep(-1, family, lambda slot: slot > done)
+    for stage, lag in enumerate((FOLD, GIVE, TAKE)):
+        for at in range(1, mid):
+            for family in range(4):
+                if at * PHASES + family > done - lag:
+                    sweep(stage, family, lambda slot, at=at, family=family: slot == at * PHASES + family)
+
     exists = ~last_line | (group <= LINE - 1 - z)
     full_from, half_from = v - group - core, v - group - 1 + core
     incoming = ends(0, 0)
@@ -584,10 +603,11 @@
             pltpu.VMEM((rows, width), f32),
             pltpu.VMEM((rows + rows // 2, width), f32),
             pltpu.VMEM((2, rows), f32),
-            pltpu.VMEM((smps, 2, rows), f32),
+            pltpu.VMEM((2 * YS, 2, rows), f32),
+            pltpu.VMEM((2, 2, rows), f32),
             pltpu.VMEM((2 * REACH + 1, 3, rows), f32),
-            dma((smps,)),
-            dma((smps,)),
+            dma((2 * YS,)),
+            dma((2 * YS,)),
             dma((4, SLOTS, CHUNKS)),
             dma((SLOTS, CHUNKS)),
             dma((2 * REACH + 1,)),
@@ -602,7 +622,7 @@
             dma((3,)),
         ],
         compiler_params=pltpu.CompilerParams(
-            collective_id=0, has_side_effects=True, vmem_limit_bytes=56 * 2**20
+            collective_id=0, has_side_effects=True, vmem_limit_bytes=38 * 2**20
         ),
         cost_estimate=pl.CostEstimate(
             flops=2 * rows * (W + rows) * cols, bytes_accessed=rows * cols * 2, transcendentals=0

time: 143 us -> 131 us (0.916)
  the two profiles are of different devices: /device:TPU:20 before, /device:TPU:27 now
where the time goes in v2:
time: 131 us; the launch traced here: 130 us
  Pallas kernels  127 us (97%)
  local copies, waits for them, and re-layouts  2.43 us (2%)
    pallas_call x1, Pallas kernels, per_device(): pl.pallas_call(functools.partial(kernel, cols * smps, rows * blocks), out...  127 us

profile of v2, /device:TPU:27, one launch (start us, length us, event | category | flops | bytes accessed | tf_op | source)
XLA Modules:
  0.0 130.4 jit_solution(10906474117622686079)
XLA Ops:
  0.6 0.7 convert_element_type.3
  1.3 0.1 broadcast_in_dim.3
  1.4 0.0 copy-start
  1.4 1.0 copy-done
  2.4 126.7 %shard_map.41 = (f32[256,128]{1,0:T(8,128)S(1)}, f32[256,128]{1,0:T(8,128)S(1)}) custom-call(bf16[256,1024]{1,0:T(8,128)(2,1)S(1)} %copy-done, f32[1,256]{1,0:T(1,128)S(1)} %bitcast.1), custom_call_target="tpu_custom_call" | custom-call | flops 1207959552 | bytes 524288 | tf_op jit(solution)/shard_map/pallas_call | solution.py:589
  129.1 0.7 copy.6
  129.7 0.7 copy.7
Async XLA Ops:
  1.4 1.0 copy-start

commit v3 on v2

--- a/solution.py
+++ b/solution.py
@@ -52,7 +52,7 @@
     total_samples, total_rows,
     dosages, counts, upper, lower,
     raw, ready, mine, twin, shares, part, other, across, arrived, window, stat_out, stat_in, stat_sum, facts,
-    stat_ss, stat_rs, raw_ss, raw_rs, fact_ss, fact_rs,
+    stat_ss, stat_rs, raw_ss, raw_rs, hop_rs, fact_ss, fact_rs,
     twin_ss, twin_rs, share_ss, share_rs, give_ss, give_rs, end_ss, end_rs,
 ):
     rows, cols = dosages.shape
@@ -78,6 +78,10 @@
     def plane_peer(step):
         return (v, hi * (2 * YS) + lax.rem(plane + step, 2 * YS))
 
+    own = raw.at[z]
+    fetch = pltpu.make_async_copy(dosages, own, stat_ss.at[2 * YS])
+    fetch.start()
+
     barrier = pltpu.get_barrier_semaphore()
     across_peer = (v, (1 - hi) * (2 * YS) + plane)
     pl.semaphore_signal(barrier, inc=1, device_id=across_peer, device_id_type=MESH)
@@ -97,11 +101,12 @@
     neighbours = jnp.minimum(v, REACH) + jnp.minimum(blocks - 1 - v, REACH)
 
     def send(way, slot, to_slot, k, src=None):
-        at = pl.ds(k * chunk, chunk)
+        at = pl.ds(0, rows) if k is None else pl.ds(k * chunk, chunk)
         to = (v - 1, v + 1, v - LINE, v + LINE)[way]
         return pltpu.make_async_remote_copy(
             src_ref=raw.at[slot, at] if src is None else src.at[at], dst_ref=raw.at[to_slot, at],
-            send_sem=raw_ss.at[way, slot, k], recv_sem=raw_rs.at[to_slot, k],
+            send_sem=raw_ss.at[to_slot],
+            recv_sem=raw_rs.at[to_slot, 0 if k is None else k] if way in (DOWN, UP) else hop_rs.at[to_slot - LINE],
             device_id=(to, s), device_id_type=MESH)
 
     def receive(slot, k):
@@ -170,7 +175,8 @@
         copy.wait_send()
 
     def local_statistics():
-        values = dosages[...].astype(f32)
+        fetch.wait()
+        values = own[...].astype(f32)
         local_mean = jnp.sum(values, axis=1, keepdims=True) / cols
         centred = values - local_mean
         local_m2 = jnp.sum(centred * centred, axis=1, keepdims=True)
@@ -254,10 +260,15 @@
     def settle():
         far_stat().wait()
         mean, m2 = pooled(stat_sum[...], cols * 2 * YS)
+        lane = lax.broadcasted_iota(jnp.int32, (3, rows), 1)
+        count = jnp.zeros((3, rows), jnp.int32)
+        for j in range(rows // BLK):
+            count = jnp.where(lane // BLK == j, counts[j], count)
+        count = count.astype(f32)
         scale = lax.rsqrt(m2 / total_samples + 1e-05)
-        facts[REACH] = jnp.where(place == 0, mean, jnp.where(place == 1, scale, counts[...]))
+        facts[REACH] = jnp.where(place == 0, mean, jnp.where(place == 1, scale, count))
         each_fact(start)
-        standardize(dosages, z, 0)
+        standardize(own, z, 0)
 
         @pl.when(last_line)
         def _():
@@ -265,8 +276,7 @@
 
     def take_in(slot, d, whole):
         if whole:
-            for k in range(CHUNKS):
-                receive(slot, k)
+            send(BACK, slot, slot, None).wait_recv()
         fact_copy(-d).wait_recv()
         standardize(raw.at[slot], slot, d)
 
@@ -310,7 +320,7 @@
                 holds, pick(low, i, 2 + i // 2), pick(low, z - 1 - i, z + 1 + i), pick(low, z - 1, ONE_ON),
                 pick(low, z, TWO_ON), pick(low, i, LINE - 1 - i), pick(low, -1 - i, 1 + i))
         below, at = z == mid - 1, z == mid
-        end = ((z == 1) & (i < 2)) | ((z == 2) & (i >= 2))
+        end = ((z == 0) & (i == 3)) | ((z == 1) & (i == 2)) | ((z == 2) & (i < 2))
         return (
             below | (at & ~last_line) | end, pick(below, i, pick(at, 2 + i // 2, 3)),
             pick(below, mid - 1 - i, mid + i), pick(below, mid - 1, pick(at, HIGH_ON, LINE - 1)),
@@ -347,11 +357,15 @@
 
         twin_copy(n).start()
 
+    def kept(n, g):
+        return n // mid * 2 + g // YS
+
     def share_copy(n, g):
-        peer = hi * (2 * YS) + lax.rem(g, YS) * 2 + core
+        to = lax.rem(g, YS)
         return pltpu.make_async_remote_copy(
-            src_ref=mine.at[n], dst_ref=shares.at[n, y], send_sem=share_ss.at[n],
-            recv_sem=share_rs.at[n, y], device_id=(v, peer), device_id_type=MESH)
+            src_ref=mine.at[n], dst_ref=shares.at[kept(n, g), (y + YS - to) % YS], send_sem=share_ss.at[n],
+            recv_sem=share_rs.at[kept(n, g)], device_id=(v, hi * (2 * YS) + to * 2 + core),
+            device_id_type=MESH)
 
     def fold(n, g):
         twin_copy(n).wait_recv()
@@ -359,129 +373,138 @@
 
         @pl.when(lax.rem(g, YS) == y)
         def _():
-            shares[n, y] = both
+            shares[kept(n, g), 0] = both
 
         @pl.when(lax.rem(g, YS) != y)
         def _():
             mine[n] = both
             share_copy(n, g).start()
 
-    def gather(n):
-        for step in range(1, YS):
-            source = lax.rem(y + step, YS)
-            pltpu.make_async_remote_copy(
-                src_ref=shares.at[n, source], dst_ref=shares.at[n, source], send_sem=share_ss.at[n],
-                recv_sem=share_rs.at[n, source], device_id=(v, s), device_id_type=MESH).wait_recv()
-        return jnp.sum(shares[n], axis=0)
-
-    def give_copy(n):
+    def gather(m):
+        pltpu.make_async_remote_copy(
+            src_ref=shares.at[m, 1:YS], dst_ref=shares.at[m, 1:YS], send_sem=share_ss.at[0],
+            recv_sem=share_rs.at[m], device_id=across_peer, device_id_type=MESH).wait_recv()
+        return jnp.sum(shares[m], axis=0)
+
+    def give_copy(m):
         return pltpu.make_async_remote_copy(
-            src_ref=part.at[n], dst_ref=across.at[n], send_sem=give_ss.at[n], recv_sem=give_rs.at[n],
+            src_ref=part.at[m], dst_ref=across.at[m], send_sem=give_ss.at[m], recv_sem=give_rs.at[m],
             device_id=across_peer, device_id_type=MESH)
 
-    def give(n):
-        part[n] = gather(n)
-        give_copy(n).start()
+    def give(m):
+        part[m] = gather(m)
+        give_copy(m).start()
 
     step_rows = rows // 2
     full_at = pl.ds(pl.multiple_of((1 - core) * step_rows, step_rows), rows)
     half_at = pl.ds(pl.multiple_of(core * rows, step_rows), step_rows)
     half_rows = pl.ds(pl.multiple_of((1 - core) * step_rows, step_rows), step_rows)
 
-    def ends(n, far):
+    def ends(m, far):
         places = []
         for j, (d, src, dst) in enumerate(
             (
-                (far, part.at[n], arrived),
-                (far + group + core, part.at[n], window.at[full_at]),
-                (far + group + 1 - core, part.at[n, half_rows], window.at[half_at]),
+                (far, part.at[m], arrived),
+                (far + group + core, part.at[m], window.at[full_at]),
+                (far + group + 1 - core, part.at[m, half_rows], window.at[half_at]),
             )
         ):
             copy = pltpu.make_async_remote_copy(
-                src_ref=src, dst_ref=dst, send_sem=end_ss.at[n, j], recv_sem=end_rs.at[j],
+                src_ref=src, dst_ref=dst, send_sem=end_ss.at[m // 2, j], recv_sem=end_rs.at[j],
                 device_id=(v + d, s), device_id_type=MESH)
             places.append((d, copy))
         return places
 
-    def take(n, far):
-        total = gather(n)
-        give_copy(n).wait_recv()
-        total = (total + across[n]) / total_samples
+    def take(m, far):
+        total = gather(m)
+        give_copy(m).wait_recv()
+        total = (total + across[m]) / total_samples
         offset = lax.broadcasted_iota(jnp.int32, (rows, width), 1) + s * width
         later = lax.broadcasted_iota(jnp.int32, (rows, width), 0) + (v + far) * rows + 1 + offset
         count = column(REACH + far, (2,))[:, 0:1]
         keep = (offset.astype(f32) < count) & (later < total_rows)
-        part[n] = jnp.where(keep, total, f32(0.0))
-        up_to, full_to, half_to = ends(n, far)
+        part[m] = jnp.where(keep, total, f32(0.0))
+        up_to, full_to, half_to = ends(m, far)
 
         @pl.when(up_to[0] == 0)
         def _():
-            arrived[...] = part[n]
+            arrived[...] = part[m]
 
         @pl.when(full_to[0] == 0)
         def _():
-            window[full_at, :] = part[n]
+            window[full_at, :] = part[m]
 
         @pl.when(half_to[0] == 0)
         def _():
-            window[half_at, :] = part[n, half_rows, :]
-
-        for d, copy in (up_to, full_to, half_to):
+            window[half_at, :] = part[m, half_rows, :]
+
+        for d, copy in (full_to, half_to, up_to):
 
             @pl.when(there(d))
             def _(copy=copy):
                 copy.start()
 
-    def sweep(stage, family, due):
+    def span(family, at):
+        if family == 0:
+            low_end = pick(at >= mid - 1, mid, at)
+            lo = pick(low, at - 1, at)
+            hi_ = pick(low, low_end, jnp.minimum(at + 1, LINE - 1 - z))
+            return lo, pick((at > 0) | ~low, hi_, lo)
+        if family == 1:
+            return at - 1, pick((at > 0) & (at <= jnp.minimum(z, mid - 1)) & ~first_line, at, at - 1)
+        if family == 2:
+            lo = pick(low, at, 2 * (at - 2))
+            return lo, pick(low, jnp.minimum(at + 1, z), pick(last_line | (at < 2), lo, jnp.minimum(lo + 2, LINE - 1 - z)))
+        at_mid = (z == mid) & (at >= 2) & ~last_line
+        end = (z < mid - 1) & (at == mid - 1)
+        lo = pick(z == mid - 1, at, pick(z == mid, 2 * (at - 2), pick(z == 2, 0, mid - 1 - z)))
+        return lo, lo + pick(z == mid - 1, 1, pick(at_mid, 2, pick(end, pick(z == 2, 2, 1), 0)))
+
+    def sweep(stage, family, step):
         def one(i, carry):
-            holds, at, row, left, right, g, far = task(family, i)
+            _, _, row, left, right, g, far = task(family, i)
             n = family * mid + i
-            now = holds & due(at * PHASES + family)
+            if stage == 0:
+                run(n, row, left, right)
             if stage == 1:
-                now = now & (lax.rem(g, YS) == y) & (g // YS != hi)
+                fold(n, g)
             if stage == 2:
-                now = now & (g == group)
-
-            @pl.when(now)
-            def _():
-                if stage == -1:
-                    run(n, row, left, right)
-                if stage == 0:
-                    fold(n, g)
-                if stage == 1:
-                    give(n)
-                if stage == 2:
-                    take(n, far)
+
+                @pl.when((lax.rem(g, YS) == y) & (g // YS != hi))
+                def _():
+                    give(kept(n, g))
+
+            if stage == 3:
+
+                @pl.when(g == group)
+                def _():
+                    take(kept(n, g), far)
 
             return carry
 
-        lax.fori_loop(0, mid, one, 0)
+        lo, up_to = span(family, step)
+        lax.fori_loop(lo, pick(step >= 0, up_to, lo), one, 0)
+
+    lags = (0, FOLD, GIVE, TAKE)
 
     def work(phase, step):
-        for stage, lag in enumerate((0, FOLD, GIVE, TAKE)):
-            family = (phase - lag) % PHASES
-            when = step * PHASES + phase - lag
-            sweep(stage - 1, family, lambda slot, when=when: slot == when)
-
-    local = [False, False, False]
-    for family in range(4):
-        for i in range(mid):
-            holds, _, _, _, _, g, far = task(family, jnp.int32(i))
-            for j, d in enumerate((far, far + group + core, far + group + 1 - core)):
-                local[j] = local[j] | (holds & (g == group) & (d == 0))
-
-    early = (z < 2) | (z >= LINE - 2)
-
-    @pl.when(early)
-    def _():
-        settle()
-
-    for k in range(CHUNKS):
-        relay(0, k, start, True)
-
-    @pl.when(~early)
-    def _():
-        settle()
+        for stage, lag in enumerate(lags):
+            sweep(stage, (phase - lag) % PHASES, step + (phase - lag) // PHASES)
+
+    settle_at = pick((z == 0) | (z == LINE - 1), 0, pick((z == 1) | (z == LINE - 2), CHUNKS // 2, CHUNKS))
+
+    def opening(k, carry):
+        @pl.when(k == settle_at)
+        def _():
+            settle()
+
+        @pl.when(k < CHUNKS)
+        def _():
+            relay(0, k, start, True)
+
+        return carry
+
+    lax.fori_loop(0, CHUNKS + 1, opening, 0)
 
     def stream(t, carry):
         for phase in range(PHASES):
@@ -494,17 +517,76 @@
         return carry
 
     lax.fori_loop(1, mid, stream, 0)
-    done = (mid - 1) * PHASES - BEHIND_BY - 1
+    done = (mid - 1) * PHASES - BEHIND_BY
+    tail = [(2, 2), (2, 3), (3, 3), (3, 0), (3, 1), (3, 2)]
     prepare(mid - 1)
+    for at, family in tail:
+        sweep(0, family, at)
+    for stage, lag in enumerate(lags):
+        if stage:
+            for slot in range(done - lag, done):
+                sweep(stage, slot % PHASES, slot // PHASES)
+            for at, family in tail:
+                sweep(stage, family, at)
+
+    own_sends(None, sent)
+
+    def relayed(i, carry):
+        relay(i, None, sent, False)
+        return carry
+
+    lax.fori_loop(0, mid, relayed, 0)
+    each_fact(sent)
+
+    def moved(family, act):
+        def one(i, carry):
+            holds, _, _, _, _, g, far = task(family, i)
+
+            @pl.when(holds)
+            def _():
+                act(family * mid + i, g, far)
+
+            return carry
+
+        lax.fori_loop(0, mid, one, 0)
+
+    def reduced(n, g, far):
+        twin_copy(n).wait_send()
+
+        @pl.when(lax.rem(g, YS) != y)
+        def _():
+            share_copy(n, g).wait_send()
+
+        @pl.when((lax.rem(g, YS) == y) & (g // YS != hi))
+        def _():
+            give_copy(kept(n, g)).wait_send()
+
+    def ended(n, g, far):
+        @pl.when(g == group)
+        def _():
+            for d, copy in ends(kept(n, g), far):
+
+                @pl.when(there(d))
+                def _(copy=copy):
+                    copy.wait_send()
+
     for family in range(4):
-        sweep(-1, family, lambda slot: slot > done)
-    for stage, lag in enumerate((FOLD, GIVE, TAKE)):
-        for at in range(1, mid):
-            for family in range(4):
-                if at * PHASES + family > done - lag:
-                    sweep(stage, family, lambda slot, at=at, family=family: slot == at * PHASES + family)
+        moved(family, reduced)
 
     exists = ~last_line | (group <= LINE - 1 - z)
+
+    def tile_here(before):
+        one_before = low & (z > 0) & ((group < z) | ((group == LINE - 1) & ~first_line))
+        at_once = ((z == mid - 1) & (group < mid)) | (~low & (z < LINE - 1) & (group == 0))
+        return pick(before == 1, one_before, at_once)
+
+    local = [
+        pick(low, (group >= mid - z) & (group < LINE - z), group < LINE - 1 - z)
+        | ((z == mid - 1) & (group == 0))
+        | ((z == mid) & (group == LINE - 1) & ~last_line),
+        tile_here(core),
+        tile_here(1 - core),
+    ]
     full_from, half_from = v - group - core, v - group - 1 + core
     incoming = ends(0, 0)
 
@@ -536,44 +618,8 @@
 
     lower[...] = unshear(window[...], rows)
 
-    for k in range(CHUNKS):
-        own_sends(k, sent)
-
-    def relayed(m, carry):
-        relay(m // CHUNKS, m % CHUNKS, sent, False)
-        return carry
-
-    lax.fori_loop(0, mid * CHUNKS, relayed, 0)
-    each_fact(sent)
-
     for family in range(4):
-
-        def moved(i, carry, family=family):
-            holds, _, _, _, _, g, far = task(family, i)
-            n = family * mid + i
-            in_plane = lax.rem(g, YS) == y
-
-            @pl.when(holds)
-            def _():
-                twin_copy(n).wait_send()
-
-            @pl.when(holds & ~in_plane)
-            def _():
-                share_copy(n, g).wait_send()
-
-            @pl.when(holds & in_plane & (g // YS != hi))
-            def _():
-                give_copy(n).wait_send()
-
-            for d, copy in ends(n, far):
-
-                @pl.when(holds & (g == group) & there(d))
-                def _(copy=copy):
-                    copy.wait_send()
-
-            return carry
-
-        lax.fori_loop(0, mid, moved, 0)
+        moved(family, ended)
 
 
 def per_device(dosages, band_counts):
@@ -581,53 +627,54 @@
     smps, blocks = lax.axis_size("smp"), lax.axis_size("var")
     width = W // smps
     f32 = jnp.float32
-    counts = jnp.repeat(band_counts.astype(f32), BLK)[None, :]
     vmem = pl.BlockSpec(memory_space=pltpu.VMEM)
     dma = pltpu.SemaphoreType.DMA
     out = jax.ShapeDtypeStruct((rows, width), f32)
-    tile = pltpu.VMEM((TASKS, rows, width), f32)
+    tiles = pltpu.VMEM((TASKS, rows, width), f32)
+    sums = pltpu.VMEM((8, rows, width), f32)
     return pl.pallas_call(
         functools.partial(kernel, cols * smps, rows * blocks),
         out_shape=(out, out),
-        in_specs=[vmem, vmem],
+        in_specs=[pl.BlockSpec(memory_space=pl.ANY), pl.BlockSpec(memory_space=pltpu.SMEM)],
         out_specs=(vmem, vmem),
         scratch_shapes=[
             pltpu.VMEM((SLOTS, rows, cols), jnp.bfloat16),
             pltpu.VMEM((SLOTS, rows, cols), jnp.bfloat16),
-            tile,
-            tile,
-            pltpu.VMEM((TASKS, YS, rows, width), f32),
-            tile,
-            tile,
-            tile,
+            tiles,
+            tiles,
+            pltpu.VMEM((8, YS, rows, width), f32),
+            sums,
+            tiles,
+            sums,
             pltpu.VMEM((rows, width), f32),
             pltpu.VMEM((rows + rows // 2, width), f32),
             pltpu.VMEM((2, rows), f32),
             pltpu.VMEM((2 * YS, 2, rows), f32),
             pltpu.VMEM((2, 2, rows), f32),
             pltpu.VMEM((2 * REACH + 1, 3, rows), f32),
+            dma((2 * YS + 1,)),
             dma((2 * YS,)),
-            dma((2 * YS,)),
-            dma((4, SLOTS, CHUNKS)),
-            dma((SLOTS, CHUNKS)),
+            dma((SLOTS,)),
+            dma((LINE, CHUNKS)),
+            dma((SLOTS - LINE,)),
             dma((2 * REACH + 1,)),
             dma((2 * REACH + 1,)),
             dma((TASKS,)),
             dma((TASKS,)),
             dma((TASKS,)),
-            dma((TASKS, YS)),
-            dma((TASKS,)),
-            dma((TASKS,)),
-            dma((TASKS, 3)),
+            dma((8,)),
+            dma((8,)),
+            dma((8,)),
+            dma((4, 3)),
             dma((3,)),
         ],
         compiler_params=pltpu.CompilerParams(
-            collective_id=0, has_side_effects=True, vmem_limit_bytes=38 * 2**20
+            collective_id=0, has_side_effects=True, vmem_limit_bytes=32 * 2**20
         ),
         cost_estimate=pl.CostEstimate(
             flops=2 * rows * (W + rows) * cols, bytes_accessed=rows * cols * 2, transcendentals=0
         ),
-    )(dosages, counts)
+    )(dosages, band_counts)
 
 
 def solution(mesh):

time: 131 us -> 122 us (0.931)
  the two profiles are of different devices: /device:TPU:27 before, /device:TPU:10 now
where the time goes in v3:
time: 122 us
  Pallas kernels  119 us (98%)
  local copies, waits for them, and re-layouts  3 us (2%)
    pallas_call x1, Pallas kernels, per_device(): pl.pallas_call(functools.partial(kernel, cols * smps, rows * blocks), out...  119 us
    unnamed x6, local copies, waits for them, and re-layouts  3 us

profile of v3, /device:TPU:10, one launch (start us, length us, event | category | flops | bytes accessed | tf_op | source)
XLA Modules:
  0.0 122.2 jit_solution(8030844508824580013)
XLA Ops:
  0.6 0.0 copy-start
  0.6 1.0 copy-done
  1.7 0.0 copy-start.1
  1.7 0.7 copy-done.1
  2.3 118.6 %shard_map.41 = (f32[256,128]{1,0:T(8,128)S(1)}, f32[256,128]{1,0:T(8,128)S(1)}) custom-call(bf16[256,1024]{1,0:T(8,128)(2,1)S(1)} %copy-done, s32[2]{0:T(128)S(1)} %copy-done.1), custom_call_target="tpu_custom_call" | custom-call | flops 1207959552 | bytes 524288 | tf_op jit(solution)/shard_map/pallas_call | solution.py:635
  120.9 0.7 copy.6
  121.6 0.7 copy.7
Async XLA Ops:
  0.6 1.0 copy-start
  1.7 0.7 copy-start.1

commit v4 on v3

--- a/solution.py
+++ b/solution.py
@@ -12,7 +12,7 @@
 LINE = 8
 YS = 4
 CHUNKS = 8
-FOLD, GIVE, TAKE = 1, 3, 6
+FOLD, GIVE, TAKE = 1, 3, 9
 BEHIND_BY = 2
 MESH = pl.DeviceIdType.MESH
 
@@ -518,7 +518,7 @@
 
     lax.fori_loop(1, mid, stream, 0)
     done = (mid - 1) * PHASES - BEHIND_BY
-    tail = [(2, 2), (2, 3), (3, 3), (3, 0), (3, 1), (3, 2)]
+    tail = [(3, 1), (3, 0), (2, 2), (2, 3), (3, 3), (3, 2)]
     prepare(mid - 1)
     for at, family in tail:
         sweep(0, family, at)

time: 122 us -> 121 us (level)
  the two profiles are of different devices: /device:TPU:10 before, /device:TPU:50 now
where the time goes in v4:
time: 121 us
  Pallas kernels  117 us (97%)
  local copies, waits for them, and re-layouts  3 us (2%)
    pallas_call x1, Pallas kernels, per_device(): pl.pallas_call(functools.partial(kernel, cols * smps, rows * blocks), out...  117 us
    unnamed x6, local copies, waits for them, and re-layouts  3 us

profile of v4, /device:TPU:50, one launch (start us, length us, event | category | flops | bytes accessed | tf_op | source)
XLA Modules:
  0.0 120.6 jit_solution(9773702888750822108)
XLA Ops:
  0.6 0.0 copy-start
  0.6 1.0 copy-done
  1.7 0.0 copy-start.1
  1.7 0.7 copy-done.1
  2.3 117.0 %shard_map.41 = (f32[256,128]{1,0:T(8,128)S(1)}, f32[256,128]{1,0:T(8,128)S(1)}) custom-call(bf16[256,1024]{1,0:T(8,128)(2,1)S(1)} %copy-done, s32[2]{0:T(128)S(1)} %copy-done.1), custom_call_target="tpu_custom_call" | custom-call | flops 1207959552 | bytes 524288 | tf_op jit(solution)/shard_map/pallas_call | solution.py:635
  119.3 0.7 copy.6
  120.0 0.7 copy.7
Async XLA Ops:
  0.6 1.0 copy-start
  1.7 0.7 copy-start.1

commit v5 on v4

--- a/solution.py
+++ b/solution.py
@@ -184,12 +184,18 @@
         both = jnp.where(lane == 0, local_mean, jnp.where(lane == 1, local_m2, f32(0.0)))
         stat_out[...] = both.T[0:2, :]
 
+    @pl.when(hi == 0)
+    def _():
+        local_statistics()
+
     pl.semaphore_wait(barrier, neighbours + 2 * YS)
 
     for k in range(CHUNKS):
         own_sends(k, start)
 
-    local_statistics()
+    @pl.when(hi != 0)
+    def _():
+        local_statistics()
 
     def stat_copy(step):
         return pltpu.make_async_remote_copy(
@@ -518,7 +524,7 @@
 
     lax.fori_loop(1, mid, stream, 0)
     done = (mid - 1) * PHASES - BEHIND_BY
-    tail = [(3, 1), (3, 0), (2, 2), (2, 3), (3, 3), (3, 2)]
+    tail = [(3, 1), (2, 2), (2, 3), (3, 3), (3, 0), (3, 2)]
     prepare(mid - 1)
     for at, family in tail:
         sweep(0, family, at)

time: 121 us -> 121 us (level)
  no operation moved by 1% of the time
where the time goes in v5:
time: 121 us; the launch traced here: 120 us
  Pallas kernels  117 us (97%)
  local copies, waits for them, and re-layouts  3 us (2%)
    pallas_call x1, Pallas kernels, per_device(): pl.pallas_call(functools.partial(kernel, cols * smps, rows * blocks), out...  117 us
    unnamed x6, local copies, waits for them, and re-layouts  3 us

profile of v5, /device:TPU:50, one launch (start us, length us, event | category | flops | bytes accessed | tf_op | source)
XLA Modules:
  0.0 120.4 jit_solution(9590895592698070754)
XLA Ops:
  0.6 0.0 copy-start
  0.6 1.0 copy-done
  1.7 0.0 copy-start.1
  1.7 0.7 copy-done.1
  2.3 116.8 %shard_map.41 = (f32[256,128]{1,0:T(8,128)S(1)}, f32[256,128]{1,0:T(8,128)S(1)}) custom-call(bf16[256,1024]{1,0:T(8,128)(2,1)S(1)} %copy-done, s32[2]{0:T(128)S(1)} %copy-done.1), custom_call_target="tpu_custom_call" | custom-call | flops 1207959552 | bytes 524288 | tf_op jit(solution)/shard_map/pallas_call | solution.py:641
  119.1 0.7 copy.6
  119.8 0.7 copy.7
Async XLA Ops:
  0.6 1.0 copy-start
  1.7 0.7 copy-start.1
